TPU v7x, 32 devices: a whole 2x2x4 slice. The times are simulated.
32 devices in a mesh: row: 8 (over z, x), sub: 4 (over y, core).
Axes of the slice: x: 2, y: 2, z: 4, core: 2. Of those that a mesh axis runs over, the one named last changes fastest.
Arguments:
- blocks: bfloat16 [256, 512, 512], P(('row', 'sub')), may hold values from 0.099 to 10
- blk_row: int32 [256], P(('row', 'sub')), may hold values from 0 to 63, as said below
- blk_col: int32 [256], P(('row', 'sub')), may hold values from 0 to 63, as said below
- counts: int32 [32], P(('row', 'sub')), may hold values from 0 to 8, as said below
- bias: float32 [32768], P(('row', 'sub')), may hold values from 0.3 to 5.1
- mask: int32 [32768], P(('row', 'sub')), may hold values 0 or 1
Outputs:
- balanced: float32 [32768], P(('row', 'sub'))
- coverage: float32 [32768], P(('row', 'sub'))
Inputs may be any that keep to these rules, and one draw needn't show every extreme that they name: blk_col equals blk_row or blk_row + 1. Among the live slots of the 4 devices of row group g, every pair (p, p) and (p, p + 1) with g * 8 <= p < (g + 1) * 8 and p + 1 < 64 stands exactly once, and no other pair; every slot, live or not, names a block row of its own group. `blk_col`: block column of each slot, as described for blk_row. `counts`: in every row group one device holds exactly 8 live slots.
All inputs are finite; a program needn't handle non-finite values. No bound on the sum of `mask` on one device may be relied on, other than what follows from the above.
Results may differ from a plain program's by a relative error of at most 0.0003.
Values sent between devices are 32-bit elements; how exact they have to be, the bound alone decides.
A program may use at most 64 MiB of HBM per device.

v0:
```python
import functools

import jax
import jax.numpy as jnp
from jax import lax
from jax.experimental import pallas as pl
from jax.experimental.pallas import tpu as pltpu
from jax.sharding import PartitionSpec as P

BLK = 512
ITERS = 3
LANES = 128
PIECES = BLK // LANES
TILE = 8
PAD = 16
LEAD = TILE


def kernel(
    row_hbm, col_hbm, count_hbm, bias_hbm, mask_hbm, blocks_ref, both_ref,
    row_ref, col_ref, count_ref, bias_ref, mask_ref, held, turned, weights, follow, part, peers, before, after, last_peers, last_before, sums_out, sums_in, mask_a, mask_c, mask_r,
    small_sem, load_sem, gather_send, gather_recv, edge_send, edge_recv, peer_send, peer_recv,
    before_send, before_recv, after_send, after_recv, sums_send, sums_recv,
):
    rows, subs = lax.axis_size("row"), lax.axis_size("sub")
    devices = rows * subs
    row, sub = lax.axis_index("row"), lax.axis_index("sub")
    me = row * subs + sub
    slots = held.shape[0]
    own = bias_ref.shape[0]
    group = own * subs
    span = group + TILE
    has_before, has_after = row > 0, row < rows - 1

    def remote(src, dst, send, recv, target_row, target_sub):
        return pltpu.make_async_remote_copy(
            src_ref=src, dst_ref=dst, send_sem=send, recv_sem=recv,
            device_id=(target_row, target_sub), device_id_type=pl.DeviceIdType.MESH,
        )

    def wait_bytes(ref, sem):
        pltpu.make_async_copy(ref, ref, sem).wait()

    def ring(offset):
        return lax.rem(sub + offset, subs)

    loads = [pltpu.make_async_copy(blocks_ref.at[s], held.at[s], load_sem.at[s]) for s in range(slots)]
    smalls = [
        pltpu.make_async_copy(src, dst, small_sem.at[i])
        for i, (src, dst) in enumerate(
            ((bias_hbm, bias_ref), (mask_hbm, mask_ref), (row_hbm, row_ref), (col_hbm, col_ref), (count_hbm, count_ref))
        )
    ]
    for load in smalls + loads:
        load.start()
    barrier = pltpu.get_barrier_semaphore()

    @pl.loop(1, devices)
    def _(offset):
        target = lax.rem(me + offset, devices)
        pl.semaphore_signal(
            barrier, inc=1, device_id=(target // subs, lax.rem(target, subs)), device_id_type=pl.DeviceIdType.MESH
        )

    for load in smalls:
        load.wait()
    first_block = row * (group // PIECES)
    ids = lax.broadcasted_iota(jnp.int32, (PAD, LANES), 0)
    edge = [
        jnp.where(
            jnp.logical_and(
                s < count_ref[0],
                jnp.logical_or(row_ref[s] == first_block, col_ref[s] == first_block + group // PIECES),
            ),
            1,
            0,
        )
        for s in range(slots)
    ]
    inner_total = slots - sum(edge)
    order = [0] * slots
    inner_seen, edge_seen = 0, 0
    for s in range(slots):
        place = jnp.where(edge[s] == 1, inner_total + edge_seen, inner_seen)
        for i in range(slots):
            order[i] = order[i] + jnp.where(place == i, s, 0)
        inner_seen = inner_seen + 1 - edge[s]
        edge_seen = edge_seen + edge[s]
    for s in range(slots):
        p = row_ref[order[s]] - first_block
        q = col_ref[order[s]] - first_block
        alive = jnp.where(order[s] < count_ref[0], 1.0, 0.0).astype(jnp.float32)
        same = jnp.where(p == q, 1.0, 0.0).astype(jnp.float32)
        at_p = jnp.where(ids == p, 1.0, 0.0).astype(jnp.float32)
        at_q = jnp.where(ids == q, 1.0, 0.0).astype(jnp.float32)
        for ref, value in (
            (mask_a, at_p * (0.5 * alive * same)),
            (mask_c, at_q * (alive * (1.0 - same))),
            (mask_r, at_p * (alive * (1.0 - same))),
        ):
            value = value.astype(jnp.bfloat16)
            ref[s] = jnp.concatenate([value, value], axis=0)
    weights[0:LEAD, :] = jnp.zeros((LEAD, LANES), jnp.float32)
    rest = weights.shape[0] - LEAD - group
    weights[LEAD + group :, :] = jnp.zeros((rest, LANES), jnp.float32)

    @pl.when(jnp.logical_not(has_after))
    def _():
        follow[...] = jnp.zeros_like(follow)
        after[...] = jnp.zeros_like(after)

    @pl.when(jnp.logical_not(has_before))
    def _():
        before[...] = jnp.zeros_like(before)
        last_before[...] = jnp.zeros_like(last_before)

    @pl.when(jnp.logical_and(has_before, sub > 0))
    def _():
        last_before[...] = jnp.zeros_like(last_before)

    own_live = mask_ref[...].astype(jnp.float32)
    mine = pl.ds(pl.multiple_of(LEAD + sub * own, TILE), own)
    weights[mine, :] = bias_ref[...] * own_live

    for s in range(0, slots // 2):
        loads[s].wait()
        turned[s] = held[s].T

    pl.semaphore_wait(barrier, devices - 1)

    @pl.when(jnp.logical_and(has_before, sub == 0))
    def _():
        for target in range(subs):
            remote(
                weights.at[pl.ds(LEAD, TILE)], follow,
                edge_send.at[target], edge_recv, row - 1, target,
            ).start()

    for offset in range(1, subs):
        remote(
            weights.at[mine], weights.at[mine], gather_send.at[offset - 1], gather_recv.at[offset - 1], row, ring(offset)
        ).start()

    for s in range(slots // 2, slots):
        loads[s].wait()
        turned[s] = held[s].T

    for offset in range(1, subs):
        theirs = weights.at[pl.ds(pl.multiple_of(LEAD + ring(subs - offset) * own, TILE), own)]
        wait_bytes(theirs, gather_recv.at[offset - 1])

    top = lax.broadcasted_iota(jnp.int32, (TILE, LANES), 0) < PIECES
    current = weights[LEAD : LEAD + group, :]
    alive = current > 0.0
    totals = []
    lane = lax.broadcasted_iota(jnp.int32, (1, LANES), 1)
    kept = jnp.sum(jnp.sum(own_live, axis=0, keepdims=True), axis=1, keepdims=True)

    def operand(start):
        value = jnp.concatenate(
            [weights[pl.ds(LEAD + start + q, PAD, stride=PIECES), :] for q in range(PIECES)], axis=1
        )
        high = value.astype(jnp.bfloat16)
        low = (value - high.astype(jnp.float32)).astype(jnp.bfloat16)
        return jnp.concatenate([high, low], axis=0)

    def wide(mask):
        return jnp.concatenate([mask] * PIECES, axis=1)

    edges = min(3, slots)
    state = {}

    def edge_weights(k):
        if k == 0:

            @pl.when(has_after)
            def _():
                wait_bytes(follow, edge_recv)

            back = jnp.where(top, follow[...], 0.0)
            state["back_live"] = back > 0.0
            state["whole"] = jnp.concatenate([current, back], axis=0)
        else:

            @pl.when(has_before)
            def _():
                wait_bytes(before.at[k - 1], before_recv.at[k - 1])

            @pl.when(has_after)
            def _():
                wait_bytes(after.at[k - 1], after_recv.at[k - 1])

            sums = state["sums"]
            front = sums[:TILE] + jnp.where(top, jnp.sum(before[k - 1], axis=0), 0.0)
            back = sums[group:] + jnp.sum(after[k - 1], axis=0)
            front = jnp.where(alive[:TILE], 1.0 / front, 0.0)
            back = jnp.where(state["back_live"], 1.0 / back, 0.0)
            weights[LEAD : LEAD + TILE, :] = front
            state["whole"] = jnp.concatenate([front, state["inner"][TILE:], back], axis=0)
        weights[LEAD + group : LEAD + span, :] = back

    for k in range(ITERS):
        total = jnp.zeros((2 * PAD, BLK), jnp.float32)
        for s in range(slots):
            if s == 0:
                here, lower, upper = operand(0), operand(-PIECES), operand(PIECES)
            if s == slots - edges:
                edge_weights(k)
                here, lower, upper = operand(0), operand(-PIECES), operand(PIECES)
            on = wide(mask_a[s]) * here
            left_c = on + wide(mask_c[s]) * lower
            left_r = on + wide(mask_r[s]) * upper
            total += lax.dot_general(left_c, held[order[s]], (((1,), (0,)), ((), ())), preferred_element_type=jnp.float32)
            total += lax.dot_general(left_r, turned[order[s]], (((1,), (0,)), ((), ())), preferred_element_type=jnp.float32)
        total = total[:PAD] + total[PAD:]
        for q in range(PIECES):
            part[k, pl.ds(q, PAD, stride=PIECES), :] = total[:, q * LANES : (q + 1) * LANES]
        final = k == ITERS - 1
        edge_rows = pl.ds(group, TILE)
        if not final:
            @pl.when(has_after)
            def _():
                for offset in range(subs):
                    remote(
                        part.at[k, edge_rows], before.at[k, offset], before_send.at[k], before_recv.at[k],
                        row + 1, ring(offset),
                    ).start()

            @pl.when(has_before)
            def _():
                for offset in range(subs):
                    remote(
                        part.at[k, pl.ds(0, TILE)], after.at[k, offset], after_send.at[k], after_recv.at[k],
                        row - 1, ring(offset),
                    ).start()

            for offset in range(1, subs):
                remote(
                    part.at[k, pl.ds(0, span)], peers.at[k, offset - 1],
                    peer_send.at[k], peer_recv.at[k], row, ring(offset),
                ).start()

            product = state["whole"] * part[k, 0:span, :]
            totals.append(jnp.sum(jnp.sum(product, axis=0, keepdims=True), axis=1, keepdims=True))
            wait_bytes(peers.at[k], peer_recv.at[k])
            sums = part[k, 0:span, :]
            for offset in range(1, subs):
                sums += peers[k, offset - 1]
            state["sums"] = sums
            state["inner"] = jnp.where(alive, 1.0 / sums[:group], 0.0)
            if k == 0:
                for offset in range(1, subs):
                    wait_bytes(weights.at[mine], gather_send.at[offset - 1])

                @pl.when(jnp.logical_and(has_before, sub == 0))
                def _():
                    for target in range(subs):
                        wait_bytes(weights.at[pl.ds(LEAD, TILE)], edge_send.at[target])

            weights[LEAD : LEAD + group, :] = state["inner"]
            weights[LEAD + group : LEAD + span, :] = jnp.zeros((TILE, LANES), jnp.float32)
        else:
            product = state["whole"] * part[k, 0:span, :]
            last = jnp.sum(product, axis=0, keepdims=True)
            half = LANES // 2
            message = last + pltpu.roll(last, half, 1)
            for i, value in enumerate(totals + [kept]):
                message = jnp.where(lane == half + i, value, message)
            message = jnp.where(lane > half + ITERS - 1, 0.0, message)
            sums_out[...] = message

            @pl.loop(0, rows)
            def _(turn):
                target_row = lax.rem(2 * rows + turn - 2 - row, rows)
                for offset in range(subs):

                    @pl.when(jnp.logical_or(target_row != row, offset != 0))
                    def _():
                        remote(
                            sums_out, sums_in.at[turn * subs + offset], sums_send, sums_recv, target_row, ring(offset)
                        ).start()

            for offset in range(1, subs):
                theirs = pl.ds(pl.multiple_of(ring(offset) * own, TILE), own)
                remote(
                    part.at[k, theirs], last_peers.at[offset - 1], peer_send.at[k], peer_recv.at[k], row, ring(offset)
                ).start()

            @pl.when(has_after)
            def _():
                remote(
                    part.at[k, edge_rows], last_before.at[sub], before_send.at[k], before_recv.at[k], row + 1, 0
                ).start()

            wait_bytes(last_peers, peer_recv.at[k])

            @pl.when(jnp.logical_and(has_before, sub == 0))
            def _():
                wait_bytes(last_before, before_recv.at[k])

            sums = part[k, pl.ds(pl.multiple_of(sub * own, TILE), own), :] + jnp.sum(last_peers[...], axis=0)
            front = jnp.where(top, jnp.sum(last_before[...], axis=0), 0.0)
            if own > TILE:
                front = jnp.concatenate([front, jnp.zeros((own - TILE, LANES), jnp.float32)], axis=0)
            sums = sums + front
            everyone = sums_in.at[pl.ds(0, devices - 1)]
            wait_bytes(everyone, sums_recv)
            self_turn = lax.rem(2 * row + 2, rows)
            sums_in[self_turn * subs] = message
            grand = jnp.sum(sums_in[...], axis=0)
            half_sum = jnp.sum(jnp.where(lane < half, grand, 0.0), axis=1, keepdims=True)
            bins = grand[:, half + ITERS - 1 : half + ITERS]
            average = half_sum / bins
            scale = average
            for i in range(ITERS - 1):
                scale = scale * (grand[:, half + i : half + i + 1] / bins)
            now = weights[mine, :]
            both_ref[1] = now * sums / average
            both_ref[0] = jnp.where(own_live > 0.0, scale / sums, 0.0)

    for k in range(ITERS):
        final = k == ITERS - 1
        wait_bytes(last_peers if final else peers.at[k], peer_send.at[k])

        @pl.when(has_after)
        def _():
            wait_bytes(last_before.at[0] if final else before.at[k], before_send.at[k])

        if not final:

            @pl.when(has_before)
            def _():
                wait_bytes(after.at[k], after_send.at[k])

    wait_bytes(sums_in.at[pl.ds(0, devices - 1)], sums_send)


def shards(blocks, blk_row, blk_col, counts, bias, mask):
    rows, subs = lax.axis_size("row"), lax.axis_size("sub")
    slots = blocks.shape[0]
    own = bias.shape[0] // LANES
    group = own * subs
    span = group + TILE
    mid = ITERS - 1
    f32, bf16 = jnp.float32, jnp.bfloat16
    dma = pltpu.SemaphoreType.DMA
    vmem = pl.BlockSpec(memory_space=pltpu.VMEM)
    both = pl.pallas_call(
        kernel,
        out_shape=jax.ShapeDtypeStruct((2, own, LANES), f32),
        in_specs=[pl.BlockSpec(memory_space=pltpu.HBM)] * 6,
        out_specs=vmem,
        scratch_shapes=[
            pltpu.SMEM((slots,), jnp.int32),
            pltpu.SMEM((slots,), jnp.int32),
            pltpu.SMEM((1,), jnp.int32),
            pltpu.VMEM((own, LANES), f32),
            pltpu.VMEM((own, LANES), jnp.int32),
            pltpu.VMEM(blocks.shape, bf16),
            pltpu.VMEM(blocks.shape, bf16),
            pltpu.VMEM((LEAD + PAD * PIECES + TILE, LANES), f32),
            pltpu.VMEM((TILE, LANES), f32),
            pltpu.VMEM((ITERS, PAD * PIECES, LANES), f32),
            pltpu.VMEM((mid, subs - 1, span, LANES), f32),
            pltpu.VMEM((mid, subs, TILE, LANES), f32),
            pltpu.VMEM((mid, subs, TILE, LANES), f32),
            pltpu.VMEM((subs - 1, own, LANES), f32),
            pltpu.VMEM((subs, TILE, LANES), f32),
            pltpu.VMEM((1, LANES), f32),
            pltpu.VMEM((rows * subs, 1, LANES), f32),
            pltpu.VMEM((slots, 2 * PAD, LANES), bf16),
            pltpu.VMEM((slots, 2 * PAD, LANES), bf16),
            pltpu.VMEM((slots, 2 * PAD, LANES), bf16),
            dma((5,)),
            dma((slots,)),
            dma((subs - 1,)),
            dma((subs - 1,)),
            dma((subs,)),
            dma,
            dma((ITERS,)),
            dma((ITERS,)),
            dma((ITERS,)),
            dma((ITERS,)),
            dma((mid,)),
            dma((mid,)),
            dma,
            dma,
        ],
        compiler_params=pltpu.CompilerParams(
            collective_id=0, has_side_effects=True, vmem_limit_bytes=64 * 1024 * 1024
        ),
    )(blk_row, blk_col, counts, bias.reshape(own, LANES), mask.reshape(own, LANES), blocks)
    balanced, coverage = both[0], both[1]
    return balanced.reshape(-1), coverage.reshape(-1)


def solution(mesh):
    everywhere = P(("row", "sub"))
    return jax.shard_map(
        shards,
        mesh=mesh,
        in_specs=(P(("row", "sub"), None, None),) + (everywhere,) * 5,
        out_specs=(everywhere, everywhere),
        check_vma=False,
    )
```

profile of v0, /device:TPU:0, one launch (start us, length us, event | category | flops | bytes accessed | tf_op | source)
XLA Modules:
  0.0 27.1 jit_solution(16014163272143202340)
XLA Ops:
  1.3 24.6 %shard_map.77 = f32[2,8,128]{2,1,0:T(8,128)} custom-call(s32[8]{0:T(128)} %row_hbm.1, s32[8]{0:T(128)} %col_hbm.1, s32[1]{0:T(128)S(6)} %copy.8.count_hbm, f32[8,128]{1,0:T(8,128)} %bitcast.6, s32[8,128]{1,0:T(8,128)} %bitcast.7, bf16[8,512,512]{2,1,0:T(8,128)(2,1)} %blocks_ref.1), custom_call_target="tpu_custom_call" | custom-call | tf_op jit(solution)/shard_map/pallas_call | solution.py:348
  25.9 1.3 %slice_bitcast_fusion = (f32[1024]{0:T(1024)}, f32[1024]{0:T(1024)}) fusion(f32[2,8,128]{2,1,0:T(8,128)} %shard_map.77), kind=kLoop, calls=%fused_computation | loop fusion | bytes 16384 | tf_op jit(solution)/shard_map/reshape;squeeze | solution.py:394
where the time goes:
time: 27.3 us; the launch traced here: 27.1 us
  Pallas kernels  24.6 us (90%)
  local copies, waits for them, and re-layouts  1.28 us (5%)
  between operations  1.28 us (5%)
    pallas_call x1, Pallas kernels, shards(): pl.pallas_call(kernel, out_shape=jax.ShapeDtypeStruct((2, own, LANES), f3...  24.6 us
    another operation x1, local copies, waits for them, and re-layouts, shards(): return (balanced.reshape(-1), coverage.reshape(-1))  1.28 us

commit v1 on v0

--- a/solution.py
+++ b/solution.py
@@ -345,9 +345,12 @@
     f32, bf16 = jnp.float32, jnp.bfloat16
     dma = pltpu.SemaphoreType.DMA
     vmem = pl.BlockSpec(memory_space=pltpu.VMEM)
+    def pin(x):
+        return pltpu.with_memory_space_constraint(x, pltpu.HBM)
+
     both = pl.pallas_call(
         kernel,
-        out_shape=jax.ShapeDtypeStruct((2, own, LANES), f32),
+        out_shape=pltpu.VMEM((2, own, LANES), f32),
         in_specs=[pl.BlockSpec(memory_space=pltpu.HBM)] * 6,
         out_specs=vmem,
         scratch_shapes=[
@@ -387,9 +390,9 @@
             dma,
         ],
         compiler_params=pltpu.CompilerParams(
-            collective_id=0, has_side_effects=True, vmem_limit_bytes=64 * 1024 * 1024
+            collective_id=0, has_side_effects=True, vmem_limit_bytes=40 * 1024 * 1024
         ),
-    )(blk_row, blk_col, counts, bias.reshape(own, LANES), mask.reshape(own, LANES), blocks)
+    )(pin(blk_row), pin(blk_col), counts, pin(bias.reshape(own, LANES)), pin(mask.reshape(own, LANES)), pin(blocks))
     balanced, coverage = both[0], both[1]
     return balanced.reshape(-1), coverage.reshape(-1)
 

time: 27.3 us -> 26 us (0.952)
  local copies, waits for them, and re-layouts: 1.28 us -> 0.6 us
  Pallas kernels: 24.6 us -> 24 us
    another operation x1, local copies, waits for them, and re-layouts: 1.28 us -> 0.6 us  [shards(): return (balanced.reshape(-1), coverage.reshape(-1))]
    pallas_call x1, Pallas kernels: 24.6 us -> 24 us  [shards(): pl.pallas_call(kernel, out_shape=pltpu.VMEM((2, own, LANES), f32), in_spe...]
where the time goes in v1:
time: 26 us; the launch traced here: 25.9 us
  Pallas kernels  24 us (92%)
  between operations  1.28 us (5%)
  local copies, waits for them, and re-layouts  0.6 us (2%)
    pallas_call x1, Pallas kernels, shards(): pl.pallas_call(kernel, out_shape=pltpu.VMEM((2, own, LANES), f32), in_spe...  24 us
    another operation x1, local copies, waits for them, and re-layouts, shards(): return (balanced.reshape(-1), coverage.reshape(-1))  0.6 us

profile of v1, /device:TPU:0, one launch (start us, length us, event | category | flops | bytes accessed | tf_op | source)
XLA Modules:
  0.0 25.9 jit_solution(8199247267939722995)
XLA Ops:
  1.3 24.0 %shard_map.77 = f32[2,8,128]{2,1,0:T(8,128)S(1)} custom-call(s32[8]{0:T(128)} %row_hbm.1, s32[8]{0:T(128)} %col_hbm.1, s32[1]{0:T(128)S(6)} %copy.8.count_hbm, f32[8,128]{1,0:T(8,128)} %bitcast.6, s32[8,128]{1,0:T(8,128)} %bitcast.7, bf16[8,512,512]{2,1,0:T(8,128)(2,1)} %blocks_ref.1), custom_call_target="tpu_custom_call" | custom-call | tf_op jit(solution)/shard_map/pallas_call | solution.py:351
  25.3 0.6 %slice_bitcast_fusion = (f32[1024]{0:T(1024)}, f32[1024]{0:T(1024)}) fusion(f32[2,8,128]{2,1,0:T(8,128)S(1)} %shard_map.77), kind=kLoop, calls=%fused_computation | loop fusion | bytes 16384 | tf_op jit(solution)/shard_map/reshape;squeeze | solution.py:397

commit v2 on v1

v2 whole, which is shorter than its diff:
```python
import functools

import jax
import jax.numpy as jnp
from jax import lax
from jax.experimental import pallas as pl
from jax.experimental.pallas import tpu as pltpu
from jax.sharding import PartitionSpec as P

BLK = 512
ITERS = 3
LANES = 128
PIECES = BLK // LANES
TILE = 8
PAD = 16
LEAD = TILE
LATE = 2


def kernel(
    row_hbm, col_hbm, count_hbm, bias_hbm, mask_hbm, blocks_ref, both_ref,
    row_ref, col_ref, count_ref, bias_ref, mask_ref, held, turned, weights, follow, part, edge_out, peers, before, after, last_peers, last_before, sums_out, sums_in, mask_a, mask_c, mask_r,
    small_sem, load_sem, gather_send, gather_recv, edge_send, edge_recv, peer_send, peer_recv,
    before_send, before_recv, after_send, after_recv, sums_send, sums_recv, known, ready,
):
    rows, subs = lax.axis_size("row"), lax.axis_size("sub")
    devices = rows * subs
    row, sub = lax.axis_index("row"), lax.axis_index("sub")
    slots = held.shape[0]
    own = bias_ref.shape[0]
    group = own * subs
    span = group + TILE
    has_before, has_after = row > 0, row < rows - 1

    def remote(src, dst, send, recv, target_row, target_sub):
        return pltpu.make_async_remote_copy(
            src_ref=src, dst_ref=dst, send_sem=send, recv_sem=recv,
            device_id=(target_row, target_sub), device_id_type=pl.DeviceIdType.MESH,
        )

    def wait_bytes(ref, sem):
        pltpu.make_async_copy(ref, ref, sem).wait()

    def ring(offset):
        return lax.rem(sub + offset, subs)

    loads = [pltpu.make_async_copy(blocks_ref.at[s], held.at[s], load_sem.at[s]) for s in range(slots)]
    smalls = [
        pltpu.make_async_copy(src, dst, small_sem.at[i])
        for i, (src, dst) in enumerate(
            ((bias_hbm, bias_ref), (mask_hbm, mask_ref), (row_hbm, row_ref), (col_hbm, col_ref), (count_hbm, count_ref))
        )
    ]
    barrier = pltpu.get_barrier_semaphore()

    def greet(target_row, target_sub, sem=barrier):
        pl.semaphore_signal(sem, inc=1, device_id=(target_row, target_sub), device_id_type=pl.DeviceIdType.MESH)

    for load in smalls:
        load.start()
    for offset in range(1, subs):
        greet(row, ring(offset))

    @pl.when(has_after)
    def _():
        for target in range(subs):
            greet(row + 1, target)

    for load in loads:
        load.start()

    stages = (rows - 1).bit_length()

    def tell(j):
        reach = 2**j

        @pl.when(row >= reach)
        def _():
            greet(row - reach, sub, known.at[j])

        @pl.when(row + reach < rows)
        def _():
            greet(row + reach, sub, known.at[j])

    def hear(j):
        reach = 2**j
        pl.semaphore_wait(known.at[j], jnp.where(row >= reach, 1, 0) + jnp.where(row + reach < rows, 1, 0))

    weights[0:LEAD, :] = jnp.zeros((LEAD, LANES), jnp.float32)
    rest = weights.shape[0] - LEAD - group
    weights[LEAD + group :, :] = jnp.zeros((rest, LANES), jnp.float32)

    @pl.when(jnp.logical_not(has_after))
    def _():
        follow[...] = jnp.zeros_like(follow)
        after[...] = jnp.zeros_like(after)

    @pl.when(jnp.logical_not(has_before))
    def _():
        before[...] = jnp.zeros_like(before)
        last_before[...] = jnp.zeros_like(last_before)

    @pl.when(jnp.logical_and(has_before, sub > 0))
    def _():
        last_before[...] = jnp.zeros_like(last_before)

    smalls[0].wait()
    smalls[1].wait()
    own_live = mask_ref[...].astype(jnp.float32)
    mine = pl.ds(pl.multiple_of(LEAD + sub * own, TILE), own)
    weights[mine, :] = bias_ref[...] * own_live

    pl.semaphore_wait(barrier, subs - 1 + jnp.where(has_before, subs, 0))

    for offset in range(1, subs):
        remote(
            weights.at[mine], weights.at[mine], gather_send.at[offset - 1], gather_recv.at[offset - 1], row, ring(offset)
        ).start()

    @pl.when(jnp.logical_and(has_before, sub == 0))
    def _():
        for target in range(subs):
            remote(
                weights.at[pl.ds(LEAD, TILE)], follow,
                edge_send.at[target], edge_recv, row - 1, target,
            ).start()

    @pl.when(has_before)
    def _():
        greet(row - 1, sub, ready)

    for load in smalls[2:]:
        load.wait()
    first_block = row * (group // PIECES)
    next_block = first_block + group // PIECES
    ids = lax.broadcasted_iota(jnp.int32, (PAD, LANES), 0)
    leaver = 0
    for s in range(slots):
        leaves = jnp.logical_and(s < count_ref[0], col_ref[s] == next_block)
        leaver = leaver + jnp.where(leaves, s, 0)
    order = [leaver] + [jnp.where(s >= leaver, s + 1, s) for s in range(slots - 1)]
    for s in range(slots):
        p = row_ref[order[s]] - first_block
        q = col_ref[order[s]] - first_block
        alive = jnp.where(order[s] < count_ref[0], 1.0, 0.0).astype(jnp.float32)
        same = jnp.where(p == q, 1.0, 0.0).astype(jnp.float32)
        at_p = jnp.where(ids == p, 1.0, 0.0).astype(jnp.float32)
        at_q = jnp.where(ids == q, 1.0, 0.0).astype(jnp.float32)
        for ref, value in (
            (mask_a, at_p * (0.5 * alive * same)),
            (mask_c, at_q * (alive * (1.0 - same))),
            (mask_r, at_p * (alive * (1.0 - same))),
        ):
            value = value.astype(jnp.bfloat16)
            ref[s] = jnp.concatenate([value, value], axis=0)

    for s in range(slots):
        loads[s].wait()
        turned[s] = held[s].T

    for offset in range(1, subs):
        theirs = weights.at[pl.ds(pl.multiple_of(LEAD + ring(subs - offset) * own, TILE), own)]
        wait_bytes(theirs, gather_recv.at[offset - 1])

    top = lax.broadcasted_iota(jnp.int32, (TILE, LANES), 0) < PIECES
    inner = weights[LEAD : LEAD + group, :]
    alive = inner > 0.0
    totals = []
    lane = lax.broadcasted_iota(jnp.int32, (1, LANES), 1)
    kept = jnp.sum(jnp.sum(own_live, axis=0, keepdims=True), axis=1, keepdims=True)

    def operand(start):
        value = jnp.concatenate(
            [weights[pl.ds(LEAD + start + q, PAD, stride=PIECES), :] for q in range(PIECES)], axis=1
        )
        high = value.astype(jnp.bfloat16)
        low = (value - high.astype(jnp.float32)).astype(jnp.bfloat16)
        return jnp.concatenate([high, low], axis=0)

    def wide(mask):
        return jnp.concatenate([mask] * PIECES, axis=1)

    def dot(left, right):
        return lax.dot_general(left, right, (((1,), (0,)), ((), ())), preferred_element_type=jnp.float32)

    edge_rows = pl.ds(group, TILE)
    edge_blocks = TILE // PIECES
    edge_at = group // PIECES
    last_slots = min(LATE, slots - 1)

    for k in range(ITERS):
        final = k == ITERS - 1
        here, lower, upper = operand(0), operand(-PIECES), operand(PIECES)
        first = dot(wide(mask_a[0]) * here + wide(mask_c[0]) * lower, held[order[0]])
        total = first
        for s in range(1, slots):
            if s == slots - last_slots:
                if k == 0:

                    @pl.when(has_after)
                    def _():
                        wait_bytes(follow, edge_recv)

                    back = jnp.where(top, follow[...], 0.0)
                    back_live = back > 0.0
                else:

                    @pl.when(has_after)
                    def _():
                        wait_bytes(after.at[k - 1], after_recv.at[k - 1])

                    back = jnp.where(back_live, 1.0 / (back_sums + jnp.sum(after[k - 1], axis=0)), 0.0)
                weights[LEAD + group : LEAD + span, :] = back
                whole = jnp.concatenate([inner, back], axis=0)
                upper_late = operand(PIECES)
            on = wide(mask_a[s]) * here
            total += dot(on + wide(mask_c[s]) * lower, held[order[s]])
            total += dot(on + wide(mask_r[s]) * upper, turned[order[s]])
            if s == 1:
                leaving = first[edge_at : edge_at + edge_blocks] + first[PAD + edge_at : PAD + edge_at + edge_blocks]
                for q in range(PIECES):
                    edge_out[k, pl.ds(q, edge_blocks, stride=PIECES), :] = leaving[:, q * LANES : (q + 1) * LANES]

                if k == 0:

                    @pl.when(has_after)
                    def _():
                        pl.semaphore_wait(ready, 1)

                    if stages:
                        tell(0)

                @pl.when(has_after)
                def _():
                    if final:
                        remote(
                            edge_out.at[k], last_before.at[sub], before_send.at[k], before_recv.at[k], row + 1, 0
                        ).start()
                    else:
                        for offset in range(subs):
                            remote(
                                edge_out.at[k], before.at[k, offset], before_send.at[k], before_recv.at[k],
                                row + 1, ring(offset),
                            ).start()

        total += dot(wide(mask_a[0]) * here + wide(mask_r[0]) * upper_late, turned[order[0]])
        total = total[:PAD] + total[PAD:]
        for q in range(PIECES):
            part[k, pl.ds(q, PAD, stride=PIECES), :] = total[:, q * LANES : (q + 1) * LANES]
        if not final:
            for offset in range(1, subs):
                remote(
                    part.at[k, pl.ds(0, span)], peers.at[k, offset - 1],
                    peer_send.at[k], peer_recv.at[k], row, ring(offset),
                ).start()

            @pl.when(has_before)
            def _():
                for offset in range(subs):
                    remote(
                        part.at[k, pl.ds(0, TILE)], after.at[k, offset], after_send.at[k], after_recv.at[k],
                        row - 1, ring(offset),
                    ).start()

            if k < stages:
                hear(k)
            if k + 1 < stages:
                tell(k + 1)
            product = whole * part[k, 0:span, :]
            totals.append(jnp.sum(jnp.sum(product, axis=0, keepdims=True), axis=1, keepdims=True))
            if k == 0:
                for offset in range(1, subs):
                    wait_bytes(weights.at[mine], gather_send.at[offset - 1])

                @pl.when(jnp.logical_and(has_before, sub == 0))
                def _():
                    for target in range(subs):
                        wait_bytes(weights.at[pl.ds(LEAD, TILE)], edge_send.at[target])

            @pl.when(has_before)
            def _():
                wait_bytes(before.at[k], before_recv.at[k])

            wait_bytes(peers.at[k], peer_recv.at[k])
            sums = part[k, 0:span, :]
            for offset in range(1, subs):
                sums += peers[k, offset - 1]
            front = sums[:TILE] + jnp.where(top, jnp.sum(before[k], axis=0), 0.0)
            back_sums = sums[group:]
            inner = jnp.where(alive, 1.0 / jnp.concatenate([front, sums[TILE:group]], axis=0), 0.0)
            weights[LEAD : LEAD + group, :] = inner
        else:
            for j in range(k, stages):
                hear(j)
                if j + 1 < stages:
                    tell(j + 1)
            product = whole * part[k, 0:span, :]
            last = jnp.sum(product, axis=0, keepdims=True)
            half = LANES // 2
            message = last + pltpu.roll(last, half, 1)
            for i, value in enumerate(totals + [kept]):
                message = jnp.where(lane == half + i, value, message)
            message = jnp.where(lane > half + ITERS - 1, 0.0, message)
            sums_out[...] = message

            @pl.loop(0, rows)
            def _(target_row):
                @pl.when(target_row != row)
                def _():
                    remote(sums_out, sums_in.at[row * subs], sums_send, sums_recv, target_row, sub).start()

                for offset in range(1, subs):
                    remote(
                        sums_out, sums_in.at[row * subs + offset], sums_send, sums_recv, target_row, ring(offset)
                    ).start()

            for offset in range(1, subs):
                theirs = pl.ds(pl.multiple_of(ring(offset) * own, TILE), own)
                remote(
                    part.at[k, theirs], last_peers.at[offset - 1], peer_send.at[k], peer_recv.at[k], row, ring(offset)
                ).start()

            wait_bytes(last_peers, peer_recv.at[k])

            @pl.when(jnp.logical_and(has_before, sub == 0))
            def _():
                wait_bytes(last_before, before_recv.at[k])

            sums = part[k, pl.ds(pl.multiple_of(sub * own, TILE), own), :] + jnp.sum(last_peers[...], axis=0)
            front = jnp.where(top, jnp.sum(last_before[...], axis=0), 0.0)
            if own > TILE:
                front = jnp.concatenate([front, jnp.zeros((own - TILE, LANES), jnp.float32)], axis=0)
            sums = sums + front
            now = weights[mine, :]
            inverse = jnp.where(own_live > 0.0, 1.0 / sums, 0.0)
            scaled = now * sums
            everyone = sums_in.at[pl.ds(0, devices - 1)]
            wait_bytes(everyone, sums_recv)
            sums_in[row * subs] = message
            grand = jnp.sum(sums_in[...], axis=0)
            half_sum = jnp.sum(jnp.where(lane < half, grand, 0.0), axis=1, keepdims=True)
            bins = grand[:, half + ITERS - 1 : half + ITERS]
            average = half_sum / bins
            scale = average
            for i in range(ITERS - 1):
                scale = scale * (grand[:, half + i : half + i + 1] / bins)
            both_ref[1] = scaled / average
            both_ref[0] = scale * inverse

    for k in range(ITERS):
        final = k == ITERS - 1
        wait_bytes(last_peers if final else peers.at[k], peer_send.at[k])

        @pl.when(has_after)
        def _():
            wait_bytes(last_before.at[0] if final else before.at[k], before_send.at[k])

        if not final:

            @pl.when(has_before)
            def _():
                wait_bytes(after.at[k], after_send.at[k])

    wait_bytes(sums_in.at[pl.ds(0, devices - 1)], sums_send)


def shards(blocks, blk_row, blk_col, counts, bias, mask):
    rows, subs = lax.axis_size("row"), lax.axis_size("sub")
    slots = blocks.shape[0]
    own = bias.shape[0] // LANES
    group = own * subs
    span = group + TILE
    mid = ITERS - 1
    f32, bf16 = jnp.float32, jnp.bfloat16
    dma = pltpu.SemaphoreType.DMA
    vmem = pl.BlockSpec(memory_space=pltpu.VMEM)
    def pin(x):
        return pltpu.with_memory_space_constraint(x, pltpu.HBM)

    both = pl.pallas_call(
        kernel,
        out_shape=pltpu.VMEM((2, own, LANES), f32),
        in_specs=[pl.BlockSpec(memory_space=pltpu.HBM)] * 6,
        out_specs=vmem,
        scratch_shapes=[
            pltpu.SMEM((slots,), jnp.int32),
            pltpu.SMEM((slots,), jnp.int32),
            pltpu.SMEM((1,), jnp.int32),
            pltpu.VMEM((own, LANES), f32),
            pltpu.VMEM((own, LANES), jnp.int32),
            pltpu.VMEM(blocks.shape, bf16),
            pltpu.VMEM(blocks.shape, bf16),
            pltpu.VMEM((LEAD + PAD * PIECES + TILE, LANES), f32),
            pltpu.VMEM((TILE, LANES), f32),
            pltpu.VMEM((ITERS, PAD * PIECES, LANES), f32),
            pltpu.VMEM((ITERS, TILE, LANES), f32),
            pltpu.VMEM((mid, subs - 1, span, LANES), f32),
            pltpu.VMEM((mid, subs, TILE, LANES), f32),
            pltpu.VMEM((mid, subs, TILE, LANES), f32),
            pltpu.VMEM((subs - 1, own, LANES), f32),
            pltpu.VMEM((subs, TILE, LANES), f32),
            pltpu.VMEM((1, LANES), f32),
            pltpu.VMEM((rows * subs, 1, LANES), f32),
            pltpu.VMEM((slots, 2 * PAD, LANES), bf16),
            pltpu.VMEM((slots, 2 * PAD, LANES), bf16),
            pltpu.VMEM((slots, 2 * PAD, LANES), bf16),
            dma((5,)),
            dma((slots,)),
            dma((subs - 1,)),
            dma((subs - 1,)),
            dma((subs,)),
            dma,
            dma((ITERS,)),
            dma((ITERS,)),
            dma((ITERS,)),
            dma((ITERS,)),
            dma((mid,)),
            dma((mid,)),
            dma,
            dma,
            pltpu.SemaphoreType.REGULAR((max((rows - 1).bit_length(), 1),)),
            pltpu.SemaphoreType.REGULAR,
        ],
        compiler_params=pltpu.CompilerParams(
            collective_id=0, has_side_effects=True, vmem_limit_bytes=40 * 1024 * 1024
        ),
    )(pin(blk_row), pin(blk_col), counts, pin(bias.reshape(own, LANES)), pin(mask.reshape(own, LANES)), pin(blocks))
    balanced, coverage = both[0], both[1]
    return balanced.reshape(-1), coverage.reshape(-1)


def solution(mesh):
    everywhere = P(("row", "sub"))
    return jax.shard_map(
        shards,
        mesh=mesh,
        in_specs=(P(("row", "sub"), None, None),) + (everywhere,) * 5,
        out_specs=(everywhere, everywhere),
        check_vma=False,
    )
```

time: 26 us -> 25.6 us (0.985)
  Pallas kernels: 24 us -> 23.6 us
    pallas_call x1, Pallas kernels: 24 us -> 23.6 us  [shards(): pl.pallas_call(kernel, out_shape=pltpu.VMEM((2, own, LANES), f32), in_spe...]
where the time goes in v2:
time: 25.6 us; the launch traced here: 25.5 us
  Pallas kernels  23.6 us (92%)
  between operations  1.28 us (5%)
  local copies, waits for them, and re-layouts  0.6 us (2%)
    pallas_call x1, Pallas kernels, shards(): pl.pallas_call(kernel, out_shape=pltpu.VMEM((2, own, LANES), f32), in_spe...  23.6 us
    another operation x1, local copies, waits for them, and re-layouts, shards(): return (balanced.reshape(-1), coverage.reshape(-1))  0.6 us

profile of v2, /device:TPU:0, one launch (start us, length us, event | category | flops | bytes accessed | tf_op | source)
XLA Modules:
  0.0 25.5 jit_solution(4026164622134259468)
XLA Ops:
  1.3 23.6 %shard_map.77 = f32[2,8,128]{2,1,0:T(8,128)S(1)} custom-call(s32[8]{0:T(128)} %row_hbm.1, s32[8]{0:T(128)} %col_hbm.1, s32[1]{0:T(128)S(6)} %copy.8.count_hbm, f32[8,128]{1,0:T(8,128)} %bitcast.6, s32[8,128]{1,0:T(8,128)} %bitcast.7, bf16[8,512,512]{2,1,0:T(8,128)(2,1)} %blocks_ref.1), custom_call_target="tpu_custom_call" | custom-call | tf_op jit(solution)/shard_map/pallas_call | solution.py:380
  24.9 0.6 %slice_bitcast_fusion = (f32[1024]{0:T(1024)}, f32[1024]{0:T(1024)}) fusion(f32[2,8,128]{2,1,0:T(8,128)S(1)} %shard_map.77), kind=kLoop, calls=%fused_computation | loop fusion | bytes 16384 | tf_op jit(solution)/shard_map/reshape;squeeze | solution.py:429

commit v3 on v2

--- a/solution.py
+++ b/solution.py
@@ -12,14 +12,14 @@
 LANES = 128
 PIECES = BLK // LANES
 TILE = 8
-PAD = 16
+PAD = 8
 LEAD = TILE
 LATE = 2
 
 
 def kernel(
     row_hbm, col_hbm, count_hbm, bias_hbm, mask_hbm, blocks_ref, both_ref,
-    row_ref, col_ref, count_ref, bias_ref, mask_ref, held, turned, weights, follow, part, edge_out, peers, before, after, last_peers, last_before, sums_out, sums_in, mask_a, mask_c, mask_r,
+    row_ref, col_ref, count_ref, bias_ref, mask_ref, held, turned, weights, follow, part, peers, before, after, last_peers, last_before, sums_out, sums_in, mask_a, mask_c, mask_r, mask_e,
     small_sem, load_sem, gather_send, gather_recv, edge_send, edge_recv, peer_send, peer_recv,
     before_send, before_recv, after_send, after_recv, sums_send, sums_recv, known, ready,
 ):
@@ -44,6 +44,7 @@
     def ring(offset):
         return lax.rem(sub + offset, subs)
 
+    others = sorted(range(1, subs), key=lambda offset: -min(offset, subs - offset))
     loads = [pltpu.make_async_copy(blocks_ref.at[s], held.at[s], load_sem.at[s]) for s in range(slots)]
     smalls = [
         pltpu.make_async_copy(src, dst, small_sem.at[i])
@@ -56,10 +57,10 @@
     def greet(target_row, target_sub, sem=barrier):
         pl.semaphore_signal(sem, inc=1, device_id=(target_row, target_sub), device_id_type=pl.DeviceIdType.MESH)
 
+    for offset in others:
+        greet(row, ring(offset))
     for load in smalls:
         load.start()
-    for offset in range(1, subs):
-        greet(row, ring(offset))
 
     @pl.when(has_after)
     def _():
@@ -89,6 +90,8 @@
     weights[0:LEAD, :] = jnp.zeros((LEAD, LANES), jnp.float32)
     rest = weights.shape[0] - LEAD - group
     weights[LEAD + group :, :] = jnp.zeros((rest, LANES), jnp.float32)
+    for k in range(ITERS):
+        part[k, group:span, :] = jnp.zeros((TILE, LANES), jnp.float32)
 
     @pl.when(jnp.logical_not(has_after))
     def _():
@@ -112,7 +115,7 @@
 
     pl.semaphore_wait(barrier, subs - 1 + jnp.where(has_before, subs, 0))
 
-    for offset in range(1, subs):
+    for offset in others:
         remote(
             weights.at[mine], weights.at[mine], gather_send.at[offset - 1], gather_recv.at[offset - 1], row, ring(offset)
         ).start()
@@ -134,10 +137,11 @@
     first_block = row * (group // PIECES)
     next_block = first_block + group // PIECES
     ids = lax.broadcasted_iota(jnp.int32, (PAD, LANES), 0)
-    leaver = 0
+    leaver, leaving = 0, 0.0
     for s in range(slots):
         leaves = jnp.logical_and(s < count_ref[0], col_ref[s] == next_block)
         leaver = leaver + jnp.where(leaves, s, 0)
+        leaving = leaving + jnp.where(leaves, 1.0, 0.0).astype(jnp.float32)
     order = [leaver] + [jnp.where(s >= leaver, s + 1, s) for s in range(slots - 1)]
     for s in range(slots):
         p = row_ref[order[s]] - first_block
@@ -153,6 +157,8 @@
         ):
             value = value.astype(jnp.bfloat16)
             ref[s] = jnp.concatenate([value, value], axis=0)
+    value = (jnp.where(ids == group // PIECES - 1, 1.0, 0.0).astype(jnp.float32) * leaving).astype(jnp.bfloat16)
+    mask_e[...] = jnp.concatenate([value, value], axis=0)
 
     for s in range(slots):
         loads[s].wait()
@@ -184,15 +190,13 @@
         return lax.dot_general(left, right, (((1,), (0,)), ((), ())), preferred_element_type=jnp.float32)
 
     edge_rows = pl.ds(group, TILE)
-    edge_blocks = TILE // PIECES
-    edge_at = group // PIECES
     last_slots = min(LATE, slots - 1)
 
     for k in range(ITERS):
         final = k == ITERS - 1
         here, lower, upper = operand(0), operand(-PIECES), operand(PIECES)
-        first = dot(wide(mask_a[0]) * here + wide(mask_c[0]) * lower, held[order[0]])
-        total = first
+        first = dot(wide(mask_a[0] + mask_e[...]) * here + wide(mask_c[0]) * lower, held[order[0]])
+        total = first * (1.0 - leaving)
         for s in range(1, slots):
             if s == slots - last_slots:
                 if k == 0:
@@ -217,9 +221,9 @@
             total += dot(on + wide(mask_c[s]) * lower, held[order[s]])
             total += dot(on + wide(mask_r[s]) * upper, turned[order[s]])
             if s == 1:
-                leaving = first[edge_at : edge_at + edge_blocks] + first[PAD + edge_at : PAD + edge_at + edge_blocks]
+                out = (first[PAD - 1 : PAD] + first[2 * PAD - 1 : 2 * PAD]) * leaving
                 for q in range(PIECES):
-                    edge_out[k, pl.ds(q, edge_blocks, stride=PIECES), :] = leaving[:, q * LANES : (q + 1) * LANES]
+                    part[k, group + q : group + q + 1, :] = out[:, q * LANES : (q + 1) * LANES]
 
                 if k == 0:
 
@@ -234,12 +238,12 @@
                 def _():
                     if final:
                         remote(
-                            edge_out.at[k], last_before.at[sub], before_send.at[k], before_recv.at[k], row + 1, 0
+                            part.at[k, edge_rows], last_before.at[sub], before_send.at[k], before_recv.at[k], row + 1, 0
                         ).start()
                     else:
                         for offset in range(subs):
                             remote(
-                                edge_out.at[k], before.at[k, offset], before_send.at[k], before_recv.at[k],
+                                part.at[k, edge_rows], before.at[k, offset], before_send.at[k], before_recv.at[k],
                                 row + 1, ring(offset),
                             ).start()
 
@@ -248,7 +252,7 @@
         for q in range(PIECES):
             part[k, pl.ds(q, PAD, stride=PIECES), :] = total[:, q * LANES : (q + 1) * LANES]
         if not final:
-            for offset in range(1, subs):
+            for offset in others:
                 remote(
                     part.at[k, pl.ds(0, span)], peers.at[k, offset - 1],
                     peer_send.at[k], peer_recv.at[k], row, ring(offset),
@@ -290,18 +294,16 @@
             inner = jnp.where(alive, 1.0 / jnp.concatenate([front, sums[TILE:group]], axis=0), 0.0)
             weights[LEAD : LEAD + group, :] = inner
         else:
+            scalars = jnp.zeros((1, LANES), jnp.float32)
+            for i, value in enumerate(totals + [kept]):
+                scalars = jnp.where(lane == i, value, scalars)
+            sums_out[1:2, :] = scalars
             for j in range(k, stages):
                 hear(j)
                 if j + 1 < stages:
                     tell(j + 1)
             product = whole * part[k, 0:span, :]
-            last = jnp.sum(product, axis=0, keepdims=True)
-            half = LANES // 2
-            message = last + pltpu.roll(last, half, 1)
-            for i, value in enumerate(totals + [kept]):
-                message = jnp.where(lane == half + i, value, message)
-            message = jnp.where(lane > half + ITERS - 1, 0.0, message)
-            sums_out[...] = message
+            sums_out[0:1, :] = jnp.sum(product, axis=0, keepdims=True)
 
             @pl.loop(0, rows)
             def _(target_row):
@@ -314,7 +316,7 @@
                         sums_out, sums_in.at[row * subs + offset], sums_send, sums_recv, target_row, ring(offset)
                     ).start()
 
-            for offset in range(1, subs):
+            for offset in others:
                 theirs = pl.ds(pl.multiple_of(ring(offset) * own, TILE), own)
                 remote(
                     part.at[k, theirs], last_peers.at[offset - 1], peer_send.at[k], peer_recv.at[k], row, ring(offset)
@@ -336,14 +338,13 @@
             scaled = now * sums
             everyone = sums_in.at[pl.ds(0, devices - 1)]
             wait_bytes(everyone, sums_recv)
-            sums_in[row * subs] = message
+            sums_in[row * subs] = sums_out[...]
             grand = jnp.sum(sums_in[...], axis=0)
-            half_sum = jnp.sum(jnp.where(lane < half, grand, 0.0), axis=1, keepdims=True)
-            bins = grand[:, half + ITERS - 1 : half + ITERS]
-            average = half_sum / bins
+            bins = grand[1:2, ITERS - 1 : ITERS]
+            average = jnp.sum(grand[0:1], axis=1, keepdims=True) / bins
             scale = average
             for i in range(ITERS - 1):
-                scale = scale * (grand[:, half + i : half + i + 1] / bins)
+                scale = scale * (grand[1:2, i : i + 1] / bins)
             both_ref[1] = scaled / average
             both_ref[0] = scale * inverse
 
@@ -392,18 +393,18 @@
             pltpu.VMEM(blocks.shape, bf16),
             pltpu.VMEM((LEAD + PAD * PIECES + TILE, LANES), f32),
             pltpu.VMEM((TILE, LANES), f32),
-            pltpu.VMEM((ITERS, PAD * PIECES, LANES), f32),
-            pltpu.VMEM((ITERS, TILE, LANES), f32),
+            pltpu.VMEM((ITERS, span, LANES), f32),
             pltpu.VMEM((mid, subs - 1, span, LANES), f32),
             pltpu.VMEM((mid, subs, TILE, LANES), f32),
             pltpu.VMEM((mid, subs, TILE, LANES), f32),
             pltpu.VMEM((subs - 1, own, LANES), f32),
             pltpu.VMEM((subs, TILE, LANES), f32),
-            pltpu.VMEM((1, LANES), f32),
-            pltpu.VMEM((rows * subs, 1, LANES), f32),
+            pltpu.VMEM((2, LANES), f32),
+            pltpu.VMEM((rows * subs, 2, LANES), f32),
             pltpu.VMEM((slots, 2 * PAD, LANES), bf16),
             pltpu.VMEM((slots, 2 * PAD, LANES), bf16),
             pltpu.VMEM((slots, 2 * PAD, LANES), bf16),
+            pltpu.VMEM((2 * PAD, LANES), bf16),
             dma((5,)),
             dma((slots,)),
             dma((subs - 1,)),

time: 25.6 us -> 24.5 us (0.957)
  Pallas kernels: 23.6 us -> 22.4 us
    pallas_call x1, Pallas kernels: 23.6 us -> 22.4 us  [shards(): pl.pallas_call(kernel, out_shape=pltpu.VMEM((2, own, LANES), f32), in_spe...]
where the time goes in v3:
time: 24.5 us; the launch traced here: 24.3 us
  Pallas kernels  22.4 us (91%)
  between operations  1.28 us (5%)
  local copies, waits for them, and re-layouts  0.6 us (2%)
    pallas_call x1, Pallas kernels, shards(): pl.pallas_call(kernel, out_shape=pltpu.VMEM((2, own, LANES), f32), in_spe...  22.4 us
    another operation x1, local copies, waits for them, and re-layouts, shards(): return (balanced.reshape(-1), coverage.reshape(-1))  0.6 us

profile of v3, /device:TPU:0, one launch (start us, length us, event | category | flops | bytes accessed | tf_op | source)
XLA Modules:
  0.0 24.3 jit_solution(3523400807743293402)
XLA Ops:
  1.3 22.4 %shard_map.77 = f32[2,8,128]{2,1,0:T(8,128)S(1)} custom-call(s32[8]{0:T(128)} %row_hbm.1, s32[8]{0:T(128)} %col_hbm.1, s32[1]{0:T(128)S(6)} %copy.8.count_hbm, f32[8,128]{1,0:T(8,128)} %bitcast.6, s32[8,128]{1,0:T(8,128)} %bitcast.7, bf16[8,512,512]{2,1,0:T(8,128)(2,1)} %blocks_ref.1), custom_call_target="tpu_custom_call" | custom-call | tf_op jit(solution)/shard_map/pallas_call | solution.py:381
  23.7 0.6 %slice_bitcast_fusion = (f32[1024]{0:T(1024)}, f32[1024]{0:T(1024)}) fusion(f32[2,8,128]{2,1,0:T(8,128)S(1)} %shard_map.77), kind=kLoop, calls=%fused_computation | loop fusion | bytes 16384 | tf_op jit(solution)/shard_map/reshape;squeeze | solution.py:430

commit v4 on v3

--- a/solution.py
+++ b/solution.py
@@ -15,6 +15,7 @@
 PAD = 8
 LEAD = TILE
 LATE = 2
+LINK = 1
 
 
 def kernel(
@@ -64,8 +65,7 @@
 
     @pl.when(has_after)
     def _():
-        for target in range(subs):
-            greet(row + 1, target)
+        greet(row + 1, LINK)
 
     for load in loads:
         load.start()
@@ -113,24 +113,18 @@
     mine = pl.ds(pl.multiple_of(LEAD + sub * own, TILE), own)
     weights[mine, :] = bias_ref[...] * own_live
 
-    pl.semaphore_wait(barrier, subs - 1 + jnp.where(has_before, subs, 0))
+    linked = jnp.logical_and(has_before, sub == LINK)
+    pl.semaphore_wait(barrier, subs - 1 + jnp.where(linked, subs, 0))
 
     for offset in others:
         remote(
             weights.at[mine], weights.at[mine], gather_send.at[offset - 1], gather_recv.at[offset - 1], row, ring(offset)
         ).start()
 
-    @pl.when(jnp.logical_and(has_before, sub == 0))
+    @pl.when(linked)
     def _():
         for target in range(subs):
-            remote(
-                weights.at[pl.ds(LEAD, TILE)], follow,
-                edge_send.at[target], edge_recv, row - 1, target,
-            ).start()
-
-    @pl.when(has_before)
-    def _():
-        greet(row - 1, sub, ready)
+            greet(row - 1, target, ready)
 
     for load in smalls[2:]:
         load.wait()
@@ -160,13 +154,30 @@
     value = (jnp.where(ids == group // PIECES - 1, 1.0, 0.0).astype(jnp.float32) * leaving).astype(jnp.bfloat16)
     mask_e[...] = jnp.concatenate([value, value], axis=0)
 
+    first_own = weights.at[pl.ds(LEAD, own)]
+
+    @pl.when(linked)
+    def _():
+        wait_bytes(first_own, gather_recv.at[LINK - 1])
+        for target in range(subs):
+            remote(
+                weights.at[pl.ds(LEAD, TILE)], follow,
+                edge_send.at[target], edge_recv, row - 1, target,
+            ).start()
+
     for s in range(slots):
         loads[s].wait()
         turned[s] = held[s].T
 
     for offset in range(1, subs):
         theirs = weights.at[pl.ds(pl.multiple_of(LEAD + ring(subs - offset) * own, TILE), own)]
-        wait_bytes(theirs, gather_recv.at[offset - 1])
+        if offset == LINK:
+
+            @pl.when(jnp.logical_not(linked))
+            def _():
+                wait_bytes(theirs, gather_recv.at[offset - 1])
+        else:
+            wait_bytes(theirs, gather_recv.at[offset - 1])
 
     top = lax.broadcasted_iota(jnp.int32, (TILE, LANES), 0) < PIECES
     inner = weights[LEAD : LEAD + group, :]
@@ -276,7 +287,7 @@
                 for offset in range(1, subs):
                     wait_bytes(weights.at[mine], gather_send.at[offset - 1])
 
-                @pl.when(jnp.logical_and(has_before, sub == 0))
+                @pl.when(linked)
                 def _():
                     for target in range(subs):
                         wait_bytes(weights.at[pl.ds(LEAD, TILE)], edge_send.at[target])

time: 24.5 us -> 24.2 us (0.988)
  Pallas kernels: 22.4 us -> 22.1 us
    pallas_call x1, Pallas kernels: 22.4 us -> 22.1 us  [shards(): pl.pallas_call(kernel, out_shape=pltpu.VMEM((2, own, LANES), f32), in_spe...]
where the time goes in v4:
time: 24.2 us; the launch traced here: 24 us
  Pallas kernels  22.1 us (91%)
  between operations  1.28 us (5%)
  local copies, waits for them, and re-layouts  0.6 us (2%)
    pallas_call x1, Pallas kernels, shards(): pl.pallas_call(kernel, out_shape=pltpu.VMEM((2, own, LANES), f32), in_spe...  22.1 us
    another operation x1, local copies, waits for them, and re-layouts, shards(): return (balanced.reshape(-1), coverage.reshape(-1))  0.6 us

profile of v4, /device:TPU:0, one launch (start us, length us, event | category | flops | bytes accessed | tf_op | source)
XLA Modules:
  0.0 24.0 jit_solution(8225728007723908242)
XLA Ops:
  1.3 22.1 %shard_map.77 = f32[2,8,128]{2,1,0:T(8,128)S(1)} custom-call(s32[8]{0:T(128)} %row_hbm.1, s32[8]{0:T(128)} %col_hbm.1, s32[1]{0:T(128)S(6)} %copy.8.count_hbm, f32[8,128]{1,0:T(8,128)} %bitcast.6, s32[8,128]{1,0:T(8,128)} %bitcast.7, bf16[8,512,512]{2,1,0:T(8,128)(2,1)} %blocks_ref.1), custom_call_target="tpu_custom_call" | custom-call | tf_op jit(solution)/shard_map/pallas_call | solution.py:392
  23.4 0.6 %slice_bitcast_fusion = (f32[1024]{0:T(1024)}, f32[1024]{0:T(1024)}) fusion(f32[2,8,128]{2,1,0:T(8,128)S(1)} %shard_map.77), kind=kLoop, calls=%fused_computation | loop fusion | bytes 16384 | tf_op jit(solution)/shard_map/reshape;squeeze | solution.py:441

commit v5 on v4

--- a/solution.py
+++ b/solution.py
@@ -131,12 +131,21 @@
     first_block = row * (group // PIECES)
     next_block = first_block + group // PIECES
     ids = lax.broadcasted_iota(jnp.int32, (PAD, LANES), 0)
-    leaver, leaving = 0, 0.0
+    leaves, enters = [], []
     for s in range(slots):
-        leaves = jnp.logical_and(s < count_ref[0], col_ref[s] == next_block)
-        leaver = leaver + jnp.where(leaves, s, 0)
-        leaving = leaving + jnp.where(leaves, 1.0, 0.0).astype(jnp.float32)
-    order = [leaver] + [jnp.where(s >= leaver, s + 1, s) for s in range(slots - 1)]
+        lives = s < count_ref[0]
+        leaves.append(jnp.where(jnp.logical_and(lives, col_ref[s] == next_block), 1, 0))
+        enters.append(jnp.where(jnp.logical_and(lives, row_ref[s] == first_block), 1, 0))
+    leavers = sum(leaves)
+    leaving = leavers.astype(jnp.float32)
+    seen, seen_last = leavers, slots - sum(enters)
+    order = [0] * slots
+    for s in range(slots):
+        place = jnp.where(leaves[s] == 1, 0, jnp.where(enters[s] == 1, seen_last, seen))
+        for i in range(slots):
+            order[i] = order[i] + jnp.where(place == i, s, 0)
+        seen = seen + 1 - leaves[s] - enters[s]
+        seen_last = seen_last + enters[s]
     for s in range(slots):
         p = row_ref[order[s]] - first_block
         q = col_ref[order[s]] - first_block
@@ -165,8 +174,9 @@
                 edge_send.at[target], edge_recv, row - 1, target,
             ).start()
 
-    for s in range(slots):
-        loads[s].wait()
+    @pl.loop(0, slots)
+    def _(s):
+        pltpu.make_async_copy(blocks_ref.at[s], held.at[s], load_sem.at[s]).wait()
         turned[s] = held[s].T
 
     for offset in range(1, subs):
@@ -186,10 +196,13 @@
     lane = lax.broadcasted_iota(jnp.int32, (1, LANES), 1)
     kept = jnp.sum(jnp.sum(own_live, axis=0, keepdims=True), axis=1, keepdims=True)
 
-    def operand(start):
-        value = jnp.concatenate(
+    def blocked(start):
+        return jnp.concatenate(
             [weights[pl.ds(LEAD + start + q, PAD, stride=PIECES), :] for q in range(PIECES)], axis=1
         )
+
+    def operand(start):
+        value = blocked(start)
         high = value.astype(jnp.bfloat16)
         low = (value - high.astype(jnp.float32)).astype(jnp.bfloat16)
         return jnp.concatenate([high, low], axis=0)
@@ -224,10 +237,18 @@
                     def _():
                         wait_bytes(after.at[k - 1], after_recv.at[k - 1])
 
+                    @pl.when(has_before)
+                    def _():
+                        wait_bytes(before.at[k - 1], before_recv.at[k - 1])
+
                     back = jnp.where(back_live, 1.0 / (back_sums + jnp.sum(after[k - 1], axis=0)), 0.0)
+                    front = front_sums + jnp.where(top, jnp.sum(before[k - 1], axis=0), 0.0)
+                    front = jnp.where(alive[:TILE], 1.0 / front, 0.0)
+                    inner = jnp.concatenate([front, inner[TILE:]], axis=0)
+                    weights[LEAD : LEAD + TILE, :] = front
                 weights[LEAD + group : LEAD + span, :] = back
                 whole = jnp.concatenate([inner, back], axis=0)
-                upper_late = operand(PIECES)
+                here, lower, upper = operand(0), operand(-PIECES), operand(PIECES)
             on = wide(mask_a[s]) * here
             total += dot(on + wide(mask_c[s]) * lower, held[order[s]])
             total += dot(on + wide(mask_r[s]) * upper, turned[order[s]])
@@ -258,11 +279,15 @@
                                 row + 1, ring(offset),
                             ).start()
 
-        total += dot(wide(mask_a[0]) * here + wide(mask_r[0]) * upper_late, turned[order[0]])
+        total += dot(wide(mask_a[0]) * here + wide(mask_r[0]) * upper, turned[order[0]])
         total = total[:PAD] + total[PAD:]
-        for q in range(PIECES):
-            part[k, pl.ds(q, PAD, stride=PIECES), :] = total[:, q * LANES : (q + 1) * LANES]
+
+        def keep():
+            for q in range(PIECES):
+                part[k, pl.ds(q, PAD, stride=PIECES), :] = total[:, q * LANES : (q + 1) * LANES]
+
         if not final:
+            keep()
             for offset in others:
                 remote(
                     part.at[k, pl.ds(0, span)], peers.at[k, offset - 1],
@@ -292,17 +317,12 @@
                     for target in range(subs):
                         wait_bytes(weights.at[pl.ds(LEAD, TILE)], edge_send.at[target])
 
-            @pl.when(has_before)
-            def _():
-                wait_bytes(before.at[k], before_recv.at[k])
-
             wait_bytes(peers.at[k], peer_recv.at[k])
             sums = part[k, 0:span, :]
             for offset in range(1, subs):
                 sums += peers[k, offset - 1]
-            front = sums[:TILE] + jnp.where(top, jnp.sum(before[k], axis=0), 0.0)
-            back_sums = sums[group:]
-            inner = jnp.where(alive, 1.0 / jnp.concatenate([front, sums[TILE:group]], axis=0), 0.0)
+            front_sums, back_sums = sums[:TILE], sums[group:]
+            inner = jnp.where(alive, 1.0 / sums[:group], 0.0)
             weights[LEAD : LEAD + group, :] = inner
         else:
             scalars = jnp.zeros((1, LANES), jnp.float32)
@@ -313,25 +333,29 @@
                 hear(j)
                 if j + 1 < stages:
                     tell(j + 1)
-            product = whole * part[k, 0:span, :]
+            product = back * part[k, group:span, :]
+            blocked_product = blocked(0) * total
+            for q in range(PIECES):
+                product += blocked_product[:, q * LANES : (q + 1) * LANES]
             sums_out[0:1, :] = jnp.sum(product, axis=0, keepdims=True)
 
-            @pl.loop(0, rows)
-            def _(target_row):
-                @pl.when(target_row != row)
-                def _():
-                    remote(sums_out, sums_in.at[row * subs], sums_send, sums_recv, target_row, sub).start()
-
-                for offset in range(1, subs):
-                    remote(
-                        sums_out, sums_in.at[row * subs + offset], sums_send, sums_recv, target_row, ring(offset)
-                    ).start()
-
+            keep()
             for offset in others:
                 theirs = pl.ds(pl.multiple_of(ring(offset) * own, TILE), own)
                 remote(
                     part.at[k, theirs], last_peers.at[offset - 1], peer_send.at[k], peer_recv.at[k], row, ring(offset)
                 ).start()
+
+            @pl.loop(0, rows)
+            def _(target_row):
+                for offset in others:
+                    remote(
+                        sums_out, sums_in.at[row * subs + offset], sums_send, sums_recv, target_row, ring(offset)
+                    ).start()
+
+                @pl.when(target_row != row)
+                def _():
+                    remote(sums_out, sums_in.at[row * subs], sums_send, sums_recv, target_row, sub).start()
 
             wait_bytes(last_peers, peer_recv.at[k])
 
@@ -352,11 +376,11 @@
             sums_in[row * subs] = sums_out[...]
             grand = jnp.sum(sums_in[...], axis=0)
             bins = grand[1:2, ITERS - 1 : ITERS]
-            average = jnp.sum(grand[0:1], axis=1, keepdims=True) / bins
-            scale = average
+            all_scaled = jnp.sum(grand[0:1], axis=1, keepdims=True)
+            scale = all_scaled / bins
             for i in range(ITERS - 1):
                 scale = scale * (grand[1:2, i : i + 1] / bins)
-            both_ref[1] = scaled / average
+            both_ref[1] = scaled * (bins / all_scaled)
             both_ref[0] = scale * inverse
 
     for k in range(ITERS):

time: 24.2 us -> 24.2 us (level)
  no operation moved by 1% of the time
where the time goes in v5:
time: 24.2 us; the launch traced here: 24 us
  Pallas kernels  22.1 us (91%)
  between operations  1.28 us (5%)
  local copies, waits for them, and re-layouts  0.6 us (2%)
    pallas_call x1, Pallas kernels, shards(): pl.pallas_call(kernel, out_shape=pltpu.VMEM((2, own, LANES), f32), in_spe...  22.1 us
    another operation x1, local copies, waits for them, and re-layouts, shards(): return (balanced.reshape(-1), coverage.reshape(-1))  0.6 us

profile of v5, /device:TPU:0, one launch (start us, length us, event | category | flops | bytes accessed | tf_op | source)
XLA Modules:
  0.0 24.0 jit_solution(16159190143328301804)
XLA Ops:
  1.3 22.1 %shard_map.77 = f32[2,8,128]{2,1,0:T(8,128)S(1)} custom-call(s32[8]{0:T(128)} %row_hbm.1, s32[8]{0:T(128)} %col_hbm.1, s32[1]{0:T(128)S(6)} %copy.8.count_hbm, f32[8,128]{1,0:T(8,128)} %bitcast.6, s32[8,128]{1,0:T(8,128)} %bitcast.7, bf16[8,512,512]{2,1,0:T(8,128)(2,1)} %blocks_ref.1), custom_call_target="tpu_custom_call" | custom-call | tf_op jit(solution)/shard_map/pallas_call | solution.py:416
  23.4 0.6 %slice_bitcast_fusion = (f32[1024]{0:T(1024)}, f32[1024]{0:T(1024)}) fusion(f32[2,8,128]{2,1,0:T(8,128)S(1)} %shard_map.77), kind=kLoop, calls=%fused_computation | loop fusion | bytes 16384 | tf_op jit(solution)/shard_map/reshape;squeeze | solution.py:465

commit v6 on v5

--- a/solution.py
+++ b/solution.py
@@ -266,6 +266,13 @@
                     if stages:
                         tell(0)
 
+                if not final:
+                    for offset in others:
+                        remote(
+                            part.at[k, edge_rows], peers.at[k, offset - 1, edge_rows],
+                            peer_send.at[k], peer_recv.at[k], row, ring(offset),
+                        ).start()
+
                 @pl.when(has_after)
                 def _():
                     if final:
@@ -290,7 +297,7 @@
             keep()
             for offset in others:
                 remote(
-                    part.at[k, pl.ds(0, span)], peers.at[k, offset - 1],
+                    part.at[k, pl.ds(0, group)], peers.at[k, offset - 1, pl.ds(0, group)],
                     peer_send.at[k], peer_recv.at[k], row, ring(offset),
                 ).start()
 

time: 24.2 us -> 24 us (level)
  no operation moved by 1% of the time
where the time goes in v6:
time: 24 us; the launch traced here: 23.9 us
  Pallas kernels  22 us (92%)
  between operations  1.28 us (5%)
  local copies, waits for them, and re-layouts  0.6 us (2%)
    pallas_call x1, Pallas kernels, shards(): pl.pallas_call(kernel, out_shape=pltpu.VMEM((2, own, LANES), f32), in_spe...  22 us
    another operation x1, local copies, waits for them, and re-layouts, shards(): return (balanced.reshape(-1), coverage.reshape(-1))  0.6 us

profile of v6, /device:TPU:0, one launch (start us, length us, event | category | flops | bytes accessed | tf_op | source)
XLA Modules:
  0.0 23.9 jit_solution(15571102787452537862)
XLA Ops:
  1.3 22.0 %shard_map.77 = f32[2,8,128]{2,1,0:T(8,128)S(1)} custom-call(s32[8]{0:T(128)} %row_hbm.1, s32[8]{0:T(128)} %col_hbm.1, s32[1]{0:T(128)S(6)} %copy.8.count_hbm, f32[8,128]{1,0:T(8,128)} %bitcast.6, s32[8,128]{1,0:T(8,128)} %bitcast.7, bf16[8,512,512]{2,1,0:T(8,128)(2,1)} %blocks_ref.1), custom_call_target="tpu_custom_call" | custom-call | tf_op jit(solution)/shard_map/pallas_call | solution.py:423
  23.3 0.6 %slice_bitcast_fusion = (f32[1024]{0:T(1024)}, f32[1024]{0:T(1024)}) fusion(f32[2,8,128]{2,1,0:T(8,128)S(1)} %shard_map.77), kind=kLoop, calls=%fused_computation | loop fusion | bytes 16384 | tf_op jit(solution)/shard_map/reshape;squeeze | solution.py:472

commit v7 on v6

--- a/solution.py
+++ b/solution.py
@@ -379,9 +379,12 @@
             inverse = jnp.where(own_live > 0.0, 1.0 / sums, 0.0)
             scaled = now * sums
             everyone = sums_in.at[pl.ds(0, devices - 1)]
+            sums_in[row * subs] = sums_out[...]
             wait_bytes(everyone, sums_recv)
-            sums_in[row * subs] = sums_out[...]
-            grand = jnp.sum(sums_in[...], axis=0)
+            grand = [sums_in[i] for i in range(4)]
+            for i in range(4, devices):
+                grand[i % 4] = grand[i % 4] + sums_in[i]
+            grand = (grand[0] + grand[1]) + (grand[2] + grand[3])
             bins = grand[1:2, ITERS - 1 : ITERS]
             all_scaled = jnp.sum(grand[0:1], axis=1, keepdims=True)
             scale = all_scaled / bins

time: 24 us -> 24 us (level)
  no operation moved by 1% of the time
where the time goes in v7:
time: 24 us; the launch traced here: 23.8 us
  Pallas kernels  21.9 us (91%)
  between operations  1.28 us (5%)
  local copies, waits for them, and re-layouts  0.6 us (2%)
    pallas_call x1, Pallas kernels, shards(): pl.pallas_call(kernel, out_shape=pltpu.VMEM((2, own, LANES), f32), in_spe...  21.9 us
    another operation x1, local copies, waits for them, and re-layouts, shards(): return (balanced.reshape(-1), coverage.reshape(-1))  0.6 us

profile of v7, /device:TPU:0, one launch (start us, length us, event | category | flops | bytes accessed | tf_op | source)
XLA Modules:
  0.0 23.8 jit_solution(13588859461198936496)
XLA Ops:
  1.3 21.9 %shard_map.77 = f32[2,8,128]{2,1,0:T(8,128)S(1)} custom-call(s32[8]{0:T(128)} %row_hbm.1, s32[8]{0:T(128)} %col_hbm.1, s32[1]{0:T(128)S(6)} %copy.8.count_hbm, f32[8,128]{1,0:T(8,128)} %bitcast.6, s32[8,128]{1,0:T(8,128)} %bitcast.7, bf16[8,512,512]{2,1,0:T(8,128)(2,1)} %blocks_ref.1), custom_call_target="tpu_custom_call" | custom-call | tf_op jit(solution)/shard_map/pallas_call | solution.py:426
  23.2 0.6 %slice_bitcast_fusion = (f32[1024]{0:T(1024)}, f32[1024]{0:T(1024)}) fusion(f32[2,8,128]{2,1,0:T(8,128)S(1)} %shard_map.77), kind=kLoop, calls=%fused_computation | loop fusion | bytes 16384 | tf_op jit(solution)/shard_map/reshape;squeeze | solution.py:475
